TPU v7x, 32 devices: a whole 2x2x4 slice. The times are simulated.
32 devices in a mesh: seq: 8 (over z, y), kvh: 4 (over x, core).
Axes of the slice: x: 2, y: 2, z: 4, core: 2. Of those that a mesh axis runs over, the one named last changes fastest.
Arguments:
- queries: bfloat16 [512, 64, 128], P('seq', 'kvh'), may hold values from -15 to 15
- stretch_kv: bfloat16 [2, 512, 8, 128], P(None, 'seq', 'kvh'), may hold values from -15 to 15
- cache_kv: bfloat16 [2, 8, 2048, 8, 128], P(None, 'seq', None, 'kvh'), may hold values from -15 to 15
- selection: int32 [8, 512, 3], P('kvh', 'seq'), may hold values from 0 to 7, all different within a row; in each aligned block of 64 rows (0 to 63, 64 to 127, ..., all dimensions but the last counted through in order) at most 25 rows name the same one
- block_owner: int32 [8], replicated, may hold values from 0 to 7, each once
Outputs:
- attended: bfloat16 [512, 8192], P(('seq', 'kvh'))
Inputs may be any that keep to these rules, and one draw needn't show every extreme that they name: `selection`: each KV head and token names 3 different blocks. Among the 64 tokens of one index of seq, for one KV head, no block is named more than 25 times, and some block is named exactly 25 times. `block_owner`: A permutation: each storage position holds exactly one block.
All inputs are finite; a program needn't handle non-finite values.
Results may differ from a plain program's by a relative error of at most 0.0051.
Values may be sent and summed in bfloat16 or wider, within the bound.
A program may use at most 128 MiB of HBM per device.

v0:
```python
import math

import jax
import jax.numpy as jnp
from jax import lax
from jax.sharding import PartitionSpec as P

BLOCK_TOKENS = 2048


def shifted(value, axis, steps):
    count = lax.axis_size(axis)
    initial, last = (max(0, -steps), min(count, count - steps))
    return lax.ppermute(value, axis, [(source, source + steps) for source in range(initial, last)])


def absorb(carried, grouped, key_rows, value_rows, allowed, scaling):
    highest, weight_sum, accumulated = carried
    scores = (
        jnp.einsum("thgd,khd->htgk", grouped, key_rows, preferred_element_type=jnp.float32)
        * scaling
    )
    scores = jnp.where(allowed, scores, -jnp.inf)
    new_highest = jnp.maximum(highest, jnp.max(scores, axis=3))
    raw_weights = jnp.exp(scores - new_highest[..., None])
    fading = jnp.exp(highest - new_highest)
    weight_sum = weight_sum * fading + jnp.sum(raw_weights, axis=3)
    accumulated = accumulated * fading[..., None] + jnp.einsum(
        "htgk,khd->htgd",
        raw_weights.astype(jnp.bfloat16),
        value_rows,
        preferred_element_type=jnp.float32,
    )
    return (new_highest, weight_sum, accumulated)


def serve_blocks(arrived, cache_kv, scaling):
    sources, items, kv_heads, group_size, head_dim = arrived.shape
    outputs = []
    log_sums = []
    for kv_index in range(kv_heads):
        query_rows = arrived[:, :, kv_index].reshape(sources * items * group_size, head_dim)
        key_rows = cache_kv[0, 0, :, kv_index]
        value_rows = cache_kv[1, 0, :, kv_index]
        scores = (
            jnp.einsum("rd,kd->rk", query_rows, key_rows, preferred_element_type=jnp.float32)
            * scaling
        )
        highest = jnp.max(scores, axis=1, keepdims=True)
        raw_weights = jnp.exp(scores - highest)
        weight_sum = jnp.sum(raw_weights, axis=1, keepdims=True)
        blended = (
            jnp.einsum(
                "rk,kd->rd",
                raw_weights.astype(jnp.bfloat16),
                value_rows,
                preferred_element_type=jnp.float32,
            )
            / weight_sum
        )
        outputs.append(blended.astype(jnp.bfloat16).reshape(sources, items, group_size, head_dim))
        log_sums.append((highest + jnp.log(weight_sum)).reshape(sources, items, group_size))
    partial_out = jnp.stack(outputs, axis=2)
    partial_lse = jnp.stack(log_sums, axis=2)
    returned = lax.all_to_all(partial_out, "seq", split_axis=0, concat_axis=0, tiled=True)
    returned_lse = lax.all_to_all(partial_lse, "seq", split_axis=0, concat_axis=0, tiled=True)
    return (returned, returned_lse)


def per_device(queries, stretch_kv, cache_kv, selection, block_owner):
    rows_local, query_heads, head_dim = queries.shape
    kv_heads = stretch_kv.shape[2]
    group_size = query_heads // kv_heads
    top_count = selection.shape[2]
    scaling = 1.0 / math.sqrt(head_dim)
    seq_count = lax.axis_size("seq")
    capacity = max(2, top_count * rows_local // seq_count + 1)
    span_devices = min(BLOCK_TOKENS // rows_local, seq_count)
    seq_place = lax.axis_index("seq")
    grouped = queries.reshape(rows_local, kv_heads, group_size, head_dim)
    targets = block_owner[selection].reshape(kv_heads, rows_local * top_count)
    matches = (targets[:, :, None] == jnp.arange(seq_count, dtype=jnp.int32)[None, None, :]).astype(
        jnp.int32
    )
    places = jnp.sum((jnp.cumsum(matches, axis=1) - 1) * matches, axis=2)
    head_rows = jnp.arange(kv_heads, dtype=jnp.int32)[:, None]
    requested = jnp.repeat(jnp.swapaxes(grouped, 0, 1), top_count, axis=1)
    outgoing = jnp.zeros((seq_count, capacity, kv_heads, group_size, head_dim), jnp.bfloat16)
    outgoing = outgoing.at[targets, places, head_rows].set(requested)
    answers, answer_lse = serve_blocks(
        lax.all_to_all(outgoing, "seq", split_axis=0, concat_axis=0, tiled=True), cache_kv, scaling
    )
    start_state = (
        jnp.full((kv_heads, rows_local, group_size), -jnp.inf, jnp.float32),
        jnp.zeros((kv_heads, rows_local, group_size), jnp.float32),
        jnp.zeros((kv_heads, rows_local, group_size, head_dim), jnp.float32),
    )
    causal = (jnp.arange(rows_local)[None, :] <= jnp.arange(rows_local)[:, None])[None, :, None, :]
    carried = absorb(start_state, grouped, stretch_kv[0], stretch_kv[1], causal, scaling)

    def advance(turn_index, loop_state):
        inner, travelling = loop_state
        travelling = shifted(travelling, "seq", 1)
        inner = absorb(
            inner, grouped, travelling[0], travelling[1], turn_index <= seq_place, scaling
        )
        return (inner, travelling)

    carried, _ = lax.fori_loop(1, span_devices, advance, (carried, stretch_kv))
    highest, weight_sum, accumulated = carried
    own_out = accumulated / weight_sum[..., None]
    own_lse = highest + jnp.log(weight_sum)
    picked = (
        answers[targets, places, head_rows]
        .astype(jnp.float32)
        .reshape(kv_heads, rows_local, top_count, group_size, head_dim)
    )
    picked_lse = answer_lse[targets, places, head_rows].reshape(
        kv_heads, rows_local, top_count, group_size
    )
    ceiling = jnp.maximum(own_lse, jnp.max(picked_lse, axis=2))
    own_weight = jnp.exp(own_lse - ceiling)
    far_weight = jnp.exp(picked_lse - ceiling[:, :, None])
    denominator = own_weight + jnp.sum(far_weight, axis=2)
    combined = (
        own_weight[..., None] * own_out + jnp.sum(far_weight[..., None] * picked, axis=2)
    ) / denominator[..., None]
    heads_out = (
        jnp.transpose(combined, (1, 0, 2, 3))
        .astype(jnp.bfloat16)
        .reshape(rows_local, query_heads * head_dim)
    )
    return lax.all_to_all(heads_out, "kvh", split_axis=0, concat_axis=1, tiled=True)


def solution(mesh):
    placed = (
        P("seq", "kvh", None),
        P(None, "seq", "kvh", None),
        P(None, "seq", None, "kvh", None),
        P("kvh", "seq", None),
        P(),
    )
    return jax.shard_map(
        per_device, mesh=mesh, in_specs=placed, out_specs=P(("seq", "kvh"), None), check_vma=False
    )
```

profile of v0, /device:TPU:16, one launch (start us, length us, event | category | flops | bytes accessed | tf_op | source)
XLA Modules:
  0.0 189.0 jit_solution(16045033954493717968)
XLA Ops:
  0.0 0.7 compare_select_fusion
  1.1 2.7 %gather_fusion = s32[384]{0:T(512)S(1)} fusion(s32[8]{0:T(128)S(1)} %copy-done, s32[1024]{0:T(1024)S(1)} %pad_clamp_fusion), kind=kCustom, calls=%fused_computation | custom fusion | bytes 4608 | tf_op jit(solution)/shard_map/gather | solution.py:81
  4.0 1.1 reduce-window.6
  5.7 1.0 broadcast_in_dim.42
  6.7 37.2 %scatter_fusion = bf16[8,25,2,8,128]{4,3,2,1,0:T(8,128)(2,1)} fusion(bf16[8,25,2,8,128]{4,3,2,1,0:T(8,128)(2,1)} %broadcast_in_dim.42, s32[384]{0:T(512)S(1)} %reshape.189, bf16[384,8,128]{2,1,0:T(8,128)(2,1)S(1)} %bitcast.98), kind=kCustom, calls=%fused_computation.3 | custom fusion | bytes 2363904 | tf_op jit(solution)/shard_map/scatter | solution.py:89
  43.9 6.2 %all-to-all-start = ((bf16[8,25,2,8,128]{4,3,2,1,0:T(8,128)(2,1)}), bf16[8,25,2,8,128]{4,3,2,1,0:T(8,128)(2,1)S(1)}, u32[]{:S(2)}, u32[]{:S(2)}) async-start(bf16[8,25,2,8,128]{4,3,2,1,0:T(8,128)(2,1)} %scatter_fusion), calls=%async_computation | async-start | bytes 1638400 | tf_op jit(solution)/shard_map/all_to_all | solution.py:91
  50.2 1.0 copy.39
  51.2 1.3 fusion.50
  52.9 1.2 convolution_add_fusion.1
  54.1 4.4 %fusion.48 = (bf16[1,1,2048,1,128]{4,3,2,1,0:T(2,128)(2,1)}, bf16[1,1,2048,1,128]{4,3,2,1,0:T(2,128)(2,1)}, bf16[1,1,2048,1,128]{4,3,2,1,0:T(2,128)(2,1)}, bf16[1,1,2048,1,128]{4,3,2,1,0:T(2,128)(2,1)}) fusion(bf16[2,1,2048,2,128]{4,3,2,1,0:T(2,128)(2,1)S(1)} %copy-done.1), kind=kLoop, calls=%fused_computation.84 | loop fusion | bytes 4194304 | tf_op jit(solution)/shard_map/slice | solution.py:44
  58.5 9.3 %all-to-all-done = bf16[8,25,2,8,128]{4,3,2,1,0:T(8,128)(2,1)S(1)} async-done(((bf16[8,25,2,8,128]{4,3,2,1,0:T(8,128)(2,1)}), bf16[8,25,2,8,128]{4,3,2,1,0:T(8,128)(2,1)S(1)}, u32[]{:S(2)}, u32[]{:S(2)}) %all-to-all-start) | async-done | bytes 819232 | tf_op jit(solution)/shard_map/all_to_all | solution.py:91
  68.0 3.3 %multiply_reduce_fusion.1 = (f32[1600]{0:T(1024)S(1)}, f32[1600,2048]{1,0:T(8,128)S(1)}) fusion(bf16[1600,128]{1,0:T(8,128)(2,1)S(1)} %bitcast.102, bf16[1,1,2048,1,128]{4,3,2,1,0:T(2,128)(2,1)} %get-tuple-element.188), kind=kOutput, calls=%fused_computation.18 | convolution fusion | flops 845412800 | bytes 14047488 | tf_op jit(solution)/shard_map/rd,kd->rk/dot_general | solution.py:46
  71.3 2.3 %fusion.6 = f32[1600]{0:T(1024)S(1)} fusion(f32[1600,2048]{1,0:T(8,128)S(1)} %get-tuple-element.197, f32[1600]{0:T(1024)S(1)} %get-tuple-element.196), kind=kLoop, calls=%fused_computation.20 | loop fusion | flops 9828800 | bytes 13120000 | tf_op jit(solution)/shard_map/reduce_sum | solution.py:51
  73.6 3.1 %fusion.16 = bf16[1600,128]{1,0:T(8,128)(2,1)S(1)} fusion(f32[1600,2048]{1,0:T(8,128)S(1)} %get-tuple-element.197, f32[1600]{0:T(1024)S(1)} %get-tuple-element.196, bf16[1,1,2048,1,128]{4,3,2,1,0:T(2,128)(2,1)S(1)} %copy-done.5, f32[1600]{0:T(1024)S(1)} %fusion.6), kind=kOutput, calls=%fused_computation.26 | convolution fusion | flops 849100800 | bytes 14053888 | tf_op jit(solution)/shard_map/rk,kd->rd/dot_general | solution.py:53
  76.8 2.0 %multiply_reduce_fusion = (f32[1600]{0:T(1024)S(1)}, f32[1600,2048]{1,0:T(8,128)S(1)}) fusion(bf16[1600,128]{1,0:T(8,128)(2,1)S(1)} %bitcast.101, bf16[1,1,2048,1,128]{4,3,2,1,0:T(2,128)(2,1)S(1)} %copy-done.3), kind=kOutput, calls=%fused_computation.17 | convolution fusion | flops 845412800 | bytes 14047488 | tf_op jit(solution)/shard_map/rd,kd->rk/dot_general | solution.py:46
  78.7 2.3 %fusion.8 = f32[1600]{0:T(1024)S(1)} fusion(f32[1600,2048]{1,0:T(8,128)S(1)} %get-tuple-element.195, f32[1600]{0:T(1024)S(1)} %get-tuple-element.194), kind=kLoop, calls=%fused_computation.22 | loop fusion | flops 9828800 | bytes 13120000 | tf_op jit(solution)/shard_map/reduce_sum | solution.py:51
  81.1 3.0 %fusion.22 = bf16[1600,128]{1,0:T(8,128)(2,1)S(1)} fusion(f32[1600,2048]{1,0:T(8,128)S(1)} %get-tuple-element.195, f32[1600]{0:T(1024)S(1)} %get-tuple-element.194, bf16[1,1,2048,1,128]{4,3,2,1,0:T(2,128)(2,1)S(1)} %copy-done.4, f32[1600]{0:T(1024)S(1)} %fusion.8), kind=kOutput, calls=%fused_computation.28 | convolution fusion | flops 849100800 | bytes 14053888 | tf_op jit(solution)/shard_map/rk,kd->rd/dot_general | solution.py:53
  84.5 0.7 reshape.208
  85.2 6.8 %all-to-all-start.1 = ((f32[8,1,400]{2,1,0:T(1,128)}), f32[8,1,400]{2,1,0:T(1,128)S(1)}, u32[]{:S(2)}, u32[]{:S(2)}) async-start(f32[8,1,400]{2,1,0:T(1,128)} %reshape.208), calls=%async_computation.1 | async-start | bytes 32768 | tf_op jit(solution)/shard_map/all_to_all | solution.py:66
  92.0 1.0 pad_maximum_fusion
  93.0 3.2 %all-to-all-done.1 = f32[8,1,400]{2,1,0:T(1,128)S(1)} async-done(((f32[8,1,400]{2,1,0:T(1,128)}), f32[8,1,400]{2,1,0:T(1,128)S(1)}, u32[]{:S(2)}, u32[]{:S(2)}) %all-to-all-start.1) | async-done | bytes 12832 | tf_op jit(solution)/shard_map/all_to_all | solution.py:66
  96.2 5.9 %all-to-all-start.2 = ((bf16[8,25,2,8,128]{4,3,1,2,0:T(8,128)(2,1)}), bf16[8,25,2,8,128]{4,3,1,2,0:T(8,128)(2,1)S(1)}, u32[]{:S(2)}, u32[]{:S(2)}) async-start(bf16[8,25,2,8,128]{4,3,1,2,0:T(8,128)(2,1)} %pad_maximum_fusion), calls=%async_computation.2 | async-start | bytes 1638400 | tf_op jit(solution)/shard_map/all_to_all | solution.py:65
  102.6 0.7 reduce.2
  103.5 4.5 %gather_fusion.1 = f32[384,8]{1,0:T(8,128)S(1)} fusion(f32[8,25,2,8]{3,2,1,0:T(2,128)S(1)} %copy.49, s32[384]{0:T(512)S(1)} %reshape.177), kind=kCustom, calls=%fused_computation.1 | custom fusion | bytes 29184 | tf_op jit(solution)/shard_map/gather | solution.py:118
  108.3 65.6 %while.19 = (s32[]{:T(128)}, f32[2,64,8]{2,1,0:T(8,128)S(1)}, f32[2,64,8]{2,1,0:T(8,128)S(1)}, f32[2,64,8,128]{3,2,1,0:T(8,128)S(1)}, bf16[2,64,2,128]{3,1,2,0:T...) while((s32[]{:T(128)}, f32[2,64,8]{2,1,0:T(8,128)S(1)}, ...), condition=%wide.region_5.6_spmd, body=%wide.region_2.0_spmd.sunk | while | flops 34277376 | bytes 3006599 | solution.py:109
  108.3 3.4 %collective-permute-start = (bf16[2,64,2,128]{3,1,2,0:T(8,128)(2,1)S(1)}, bf16[2,64,2,128]{3,1,2,0:T(8,128)(2,1)S(1)}, u32[]{:S(2)}, u32[]{:S(2)}) collective-permute-start(bf16[2,64,2,128]{3,1,2,0:T(8,128)(2,1)S(1)} %get-tuple-element.263), channel_id=1, source_target_pairs={{0,4},{4,8},{8,12},{12,16},{16,20},{20,24},{24,28},{1,5},{5,9},{9,... | collective-permute-start | bytes 196616 | tf_op jit(solution)/shard_map/while/body/eval_jaxpr/ppermute | solution.py:14
  111.7 10.1 %collective-permute-done = bf16[2,64,2,128]{3,1,2,0:T(8,128)(2,1)S(1)} collective-permute-done((bf16[2,64,2,128]{3,1,2,0:T(8,128)(2,1)S(1)}, bf16[2,64,2,128]{3,1,2,0:T(8,128)(2,1)S(1)}, u32[]{:S(2)}, u32[]{:S(2)}) %collective-permute-start) | collective-permute-done | bytes 65568 | tf_op jit(solution)/shard_map/while/body/eval_jaxpr/ppermute | solution.py:14
  122.7 0.5 convolution_add_fusion.3
  123.3 1.9 %collective-permute-start = (bf16[2,64,2,128]{3,1,2,0:T(8,128)(2,1)S(1)}, bf16[2,64,2,128]{3,1,2,0:T(8,128)(2,1)S(1)}, u32[]{:S(2)}, u32[]{:S(2)}) collective-permute-start(bf16[2,64,2,128]{3,1,2,0:T(8,128)(2,1)S(1)} %get-tuple-element.263), channel_id=1, source_target_pairs={{0,4},{4,8},{8,12},{12,16},{16,20},{20,24},{24,28},{1,5},{5,9},{9,... | collective-permute-start | bytes 196616 | tf_op jit(solution)/shard_map/while/body/eval_jaxpr/ppermute | solution.py:14
  125.2 5.1 %collective-permute-done = bf16[2,64,2,128]{3,1,2,0:T(8,128)(2,1)S(1)} collective-permute-done((bf16[2,64,2,128]{3,1,2,0:T(8,128)(2,1)S(1)}, bf16[2,64,2,128]{3,1,2,0:T(8,128)(2,1)S(1)}, u32[]{:S(2)}, u32[]{:S(2)}) %collective-permute-start) | collective-permute-done | bytes 65568 | tf_op jit(solution)/shard_map/while/body/eval_jaxpr/ppermute | solution.py:14
  131.1 0.5 convolution_add_fusion.3
  131.7 1.9 %collective-permute-start = (bf16[2,64,2,128]{3,1,2,0:T(8,128)(2,1)S(1)}, bf16[2,64,2,128]{3,1,2,0:T(8,128)(2,1)S(1)}, u32[]{:S(2)}, u32[]{:S(2)}) collective-permute-start(bf16[2,64,2,128]{3,1,2,0:T(8,128)(2,1)S(1)} %get-tuple-element.263), channel_id=1, source_target_pairs={{0,4},{4,8},{8,12},{12,16},{16,20},{20,24},{24,28},{1,5},{5,9},{9,... | collective-permute-start | bytes 196616 | tf_op jit(solution)/shard_map/while/body/eval_jaxpr/ppermute | solution.py:14
  133.6 5.1 %collective-permute-done = bf16[2,64,2,128]{3,1,2,0:T(8,128)(2,1)S(1)} collective-permute-done((bf16[2,64,2,128]{3,1,2,0:T(8,128)(2,1)S(1)}, bf16[2,64,2,128]{3,1,2,0:T(8,128)(2,1)S(1)}, u32[]{:S(2)}, u32[]{:S(2)}) %collective-permute-start) | collective-permute-done | bytes 65568 | tf_op jit(solution)/shard_map/while/body/eval_jaxpr/ppermute | solution.py:14
  139.6 0.5 convolution_add_fusion.3
  140.1 1.9 %collective-permute-start = (bf16[2,64,2,128]{3,1,2,0:T(8,128)(2,1)S(1)}, bf16[2,64,2,128]{3,1,2,0:T(8,128)(2,1)S(1)}, u32[]{:S(2)}, u32[]{:S(2)}) collective-permute-start(bf16[2,64,2,128]{3,1,2,0:T(8,128)(2,1)S(1)} %get-tuple-element.263), channel_id=1, source_target_pairs={{0,4},{4,8},{8,12},{12,16},{16,20},{20,24},{24,28},{1,5},{5,9},{9,... | collective-permute-start | bytes 196616 | tf_op jit(solution)/shard_map/while/body/eval_jaxpr/ppermute | solution.py:14
  142.1 5.1 %collective-permute-done = bf16[2,64,2,128]{3,1,2,0:T(8,128)(2,1)S(1)} collective-permute-done((bf16[2,64,2,128]{3,1,2,0:T(8,128)(2,1)S(1)}, bf16[2,64,2,128]{3,1,2,0:T(8,128)(2,1)S(1)}, u32[]{:S(2)}, u32[]{:S(2)}) %collective-permute-start) | collective-permute-done | bytes 65568 | tf_op jit(solution)/shard_map/while/body/eval_jaxpr/ppermute | solution.py:14
  148.0 0.5 convolution_add_fusion.3
  148.6 1.9 %collective-permute-start = (bf16[2,64,2,128]{3,1,2,0:T(8,128)(2,1)S(1)}, bf16[2,64,2,128]{3,1,2,0:T(8,128)(2,1)S(1)}, u32[]{:S(2)}, u32[]{:S(2)}) collective-permute-start(bf16[2,64,2,128]{3,1,2,0:T(8,128)(2,1)S(1)} %get-tuple-element.263), channel_id=1, source_target_pairs={{0,4},{4,8},{8,12},{12,16},{16,20},{20,24},{24,28},{1,5},{5,9},{9,... | collective-permute-start | bytes 196616 | tf_op jit(solution)/shard_map/while/body/eval_jaxpr/ppermute | solution.py:14
  150.5 5.1 %collective-permute-done = bf16[2,64,2,128]{3,1,2,0:T(8,128)(2,1)S(1)} collective-permute-done((bf16[2,64,2,128]{3,1,2,0:T(8,128)(2,1)S(1)}, bf16[2,64,2,128]{3,1,2,0:T(8,128)(2,1)S(1)}, u32[]{:S(2)}, u32[]{:S(2)}) %collective-permute-start) | collective-permute-done | bytes 65568 | tf_op jit(solution)/shard_map/while/body/eval_jaxpr/ppermute | solution.py:14
  157.0 1.9 %collective-permute-start = (bf16[2,64,2,128]{3,1,2,0:T(8,128)(2,1)S(1)}, bf16[2,64,2,128]{3,1,2,0:T(8,128)(2,1)S(1)}, u32[]{:S(2)}, u32[]{:S(2)}) collective-permute-start(bf16[2,64,2,128]{3,1,2,0:T(8,128)(2,1)S(1)} %get-tuple-element.263), channel_id=1, source_target_pairs={{0,4},{4,8},{8,12},{12,16},{16,20},{20,24},{24,28},{1,5},{5,9},{9,... | collective-permute-start | bytes 196616 | tf_op jit(solution)/shard_map/while/body/eval_jaxpr/ppermute | solution.py:14
  159.0 5.1 %collective-permute-done = bf16[2,64,2,128]{3,1,2,0:T(8,128)(2,1)S(1)} collective-permute-done((bf16[2,64,2,128]{3,1,2,0:T(8,128)(2,1)S(1)}, bf16[2,64,2,128]{3,1,2,0:T(8,128)(2,1)S(1)}, u32[]{:S(2)}, u32[]{:S(2)}) %collective-permute-start) | collective-permute-done | bytes 65568 | tf_op jit(solution)/shard_map/while/body/eval_jaxpr/ppermute | solution.py:14
  164.9 0.5 convolution_add_fusion.3
  165.5 1.9 %collective-permute-start = (bf16[2,64,2,128]{3,1,2,0:T(8,128)(2,1)S(1)}, bf16[2,64,2,128]{3,1,2,0:T(8,128)(2,1)S(1)}, u32[]{:S(2)}, u32[]{:S(2)}) collective-permute-start(bf16[2,64,2,128]{3,1,2,0:T(8,128)(2,1)S(1)} %get-tuple-element.263), channel_id=1, source_target_pairs={{0,4},{4,8},{8,12},{12,16},{16,20},{20,24},{24,28},{1,5},{5,9},{9,... | collective-permute-start | bytes 196616 | tf_op jit(solution)/shard_map/while/body/eval_jaxpr/ppermute | solution.py:14
  167.4 5.1 %collective-permute-done = bf16[2,64,2,128]{3,1,2,0:T(8,128)(2,1)S(1)} collective-permute-done((bf16[2,64,2,128]{3,1,2,0:T(8,128)(2,1)S(1)}, bf16[2,64,2,128]{3,1,2,0:T(8,128)(2,1)S(1)}, u32[]{:S(2)}, u32[]{:S(2)}) %collective-permute-start) | collective-permute-done | bytes 65568 | tf_op jit(solution)/shard_map/while/body/eval_jaxpr/ppermute | solution.py:14
  173.4 0.5 convolution_add_fusion.3
  174.3 4.2 %gather_fusion.2 = bf16[384,8,128]{2,1,0:T(8,128)(2,1)S(1)} fusion(bf16[8,25,2,8,128]{4,3,1,2,0:T(8,128)(2,1)S(1)} %all-to-all-done.2, s32[384]{0:T(512)S(1)} %reshape.177), kind=kCustom, calls=%fused_computation.2 | custom fusion | bytes 1577472 | tf_op jit(solution)/shard_map/gather | solution.py:114
  179.6 8.6 %all_to_all.34 = bf16[4,16,2048]{2,1,0:T(8,128)(2,1)S(1)} all-to-all(bf16[4,16,2048]{2,1,0:T(8,128)(2,1)S(1)} %all_to_all.26), channel_id=1, replica_groups=mesh['seq'=8,'kvh'=4] {'kvh'}, dimensions={0} | all-to-all | bytes 524288 | tf_op jit(solution)/shard_map/all_to_all | solution.py:133
  188.3 0.7 copy.64
  (101 shorter events, 10.7 us)
Async XLA Ops:
  0.0 1.0 copy-start
  1.1 4.5 %copy-start.2 = (bf16[64,16,128]{2,1,0:T(8,128)(2,1)S(1)}, bf16[64,16,128]{2,1,0:T(8,128)(2,1)}, u32[]{:S(2)}) copy-start(bf16[64,16,128]{2,1,0:T(8,128)(2,1)} %param.7) | copy-start | bytes 786436
  1.1 49.1 %copy-start.7 = (bf16[2,64,2,128]{3,2,1,0:T(2,128)(2,1)S(1)}, bf16[2,64,2,128]{3,2,1,0:T(2,128)(2,1)}, u32[]{:S(2)}) copy-start(bf16[2,64,2,128]{3,2,1,0:T(2,128)(2,1)} %param.8) | copy-start | bytes 196612
  3.8 50.3 %copy-start.1 = (bf16[2,1,2048,2,128]{4,3,2,1,0:T(2,128)(2,1)S(1)}, bf16[2,1,2048,2,128]{4,3,2,1,0:T(2,128)(2,1)}, u32[]{:S(2)}) copy-start(bf16[2,1,2048,2,128]{4,3,2,1,0:T(2,128)(2,1)} %param.9) | copy-start | bytes 6291460
  43.9 23.9 %all-to-all-start = ((bf16[8,25,2,8,128]{4,3,2,1,0:T(8,128)(2,1)}), bf16[8,25,2,8,128]{4,3,2,1,0:T(8,128)(2,1)S(1)}, u32[]{:S(2)}, u32[]{:S(2)}) async-start(bf16[8,25,2,8,128]{4,3,2,1,0:T(8,128)(2,1)} %scatter_fusion), calls=%async_computation | async-start | bytes 1638400 | tf_op jit(solution)/shard_map/all_to_all | solution.py:91
  68.0 5.6 %copy-start.5 = (bf16[1,1,2048,1,128]{4,3,2,1,0:T(2,128)(2,1)S(1)}, bf16[1,1,2048,1,128]{4,3,2,1,0:T(2,128)(2,1)}, u32[]{:S(2)}) copy-start(bf16[1,1,2048,1,128]{4,3,2,1,0:T(2,128)(2,1)} %get-tuple-element.186) | copy-start | bytes 1572868
  73.6 3.2 %copy-start.3 = (bf16[1,1,2048,1,128]{4,3,2,1,0:T(2,128)(2,1)S(1)}, bf16[1,1,2048,1,128]{4,3,2,1,0:T(2,128)(2,1)}, u32[]{:S(2)}) copy-start(bf16[1,1,2048,1,128]{4,3,2,1,0:T(2,128)(2,1)} %get-tuple-element.187) | copy-start | bytes 1572868
  76.7 4.3 %copy-start.4 = (bf16[1,1,2048,1,128]{4,3,2,1,0:T(2,128)(2,1)S(1)}, bf16[1,1,2048,1,128]{4,3,2,1,0:T(2,128)(2,1)}, u32[]{:S(2)}) copy-start(bf16[1,1,2048,1,128]{4,3,2,1,0:T(2,128)(2,1)} %get-tuple-element.189) | copy-start | bytes 1572868
  81.0 27.3 %copy-start.6 = (f32[2,64,8,128]{3,2,1,0:T(8,128)S(1)}, f32[2,64,8,128]{3,2,1,0:T(8,128)}, u32[]{:S(2)}) copy-start(f32[2,64,8,128]{3,2,1,0:T(8,128)} %convolution_add_fusion.1) | copy-start | bytes 1572868
  85.2 11.0 %all-to-all-start.1 = ((f32[8,1,400]{2,1,0:T(1,128)}), f32[8,1,400]{2,1,0:T(1,128)S(1)}, u32[]{:S(2)}, u32[]{:S(2)}) async-start(f32[8,1,400]{2,1,0:T(1,128)} %reshape.208), calls=%async_computation.1 | async-start | bytes 32768 | tf_op jit(solution)/shard_map/all_to_all | solution.py:66
  96.2 78.1 %all-to-all-start.2 = ((bf16[8,25,2,8,128]{4,3,1,2,0:T(8,128)(2,1)}), bf16[8,25,2,8,128]{4,3,1,2,0:T(8,128)(2,1)S(1)}, u32[]{:S(2)}, u32[]{:S(2)}) async-start(bf16[8,25,2,8,128]{4,3,1,2,0:T(8,128)(2,1)} %pad_maximum_fusion), calls=%async_computation.2 | async-start | bytes 1638400 | tf_op jit(solution)/shard_map/all_to_all | solution.py:65
  108.3 13.5 %collective-permute-start = (bf16[2,64,2,128]{3,1,2,0:T(8,128)(2,1)S(1)}, bf16[2,64,2,128]{3,1,2,0:T(8,128)(2,1)S(1)}, u32[]{:S(2)}, u32[]{:S(2)}) collective-permute-start(bf16[2,64,2,128]{3,1,2,0:T(8,128)(2,1)S(1)} %get-tuple-element.263), channel_id=1, source_target_pairs={{0,4},{4,8},{8,12},{12,16},{16,20},{20,24},{24,28},{1,5},{5,9},{9,... | collective-permute-start | bytes 196616 | tf_op jit(solution)/shard_map/while/body/eval_jaxpr/ppermute | solution.py:14
  123.3 7.1 %collective-permute-start = (bf16[2,64,2,128]{3,1,2,0:T(8,128)(2,1)S(1)}, bf16[2,64,2,128]{3,1,2,0:T(8,128)(2,1)S(1)}, u32[]{:S(2)}, u32[]{:S(2)}) collective-permute-start(bf16[2,64,2,128]{3,1,2,0:T(8,128)(2,1)S(1)} %get-tuple-element.263), channel_id=1, source_target_pairs={{0,4},{4,8},{8,12},{12,16},{16,20},{20,24},{24,28},{1,5},{5,9},{9,... | collective-permute-start | bytes 196616 | tf_op jit(solution)/shard_map/while/body/eval_jaxpr/ppermute | solution.py:14
  131.7 7.1 %collective-permute-start = (bf16[2,64,2,128]{3,1,2,0:T(8,128)(2,1)S(1)}, bf16[2,64,2,128]{3,1,2,0:T(8,128)(2,1)S(1)}, u32[]{:S(2)}, u32[]{:S(2)}) collective-permute-start(bf16[2,64,2,128]{3,1,2,0:T(8,128)(2,1)S(1)} %get-tuple-element.263), channel_id=1, source_target_pairs={{0,4},{4,8},{8,12},{12,16},{16,20},{20,24},{24,28},{1,5},{5,9},{9,... | collective-permute-start | bytes 196616 | tf_op jit(solution)/shard_map/while/body/eval_jaxpr/ppermute | solution.py:14
  140.1 7.1 %collective-permute-start = (bf16[2,64,2,128]{3,1,2,0:T(8,128)(2,1)S(1)}, bf16[2,64,2,128]{3,1,2,0:T(8,128)(2,1)S(1)}, u32[]{:S(2)}, u32[]{:S(2)}) collective-permute-start(bf16[2,64,2,128]{3,1,2,0:T(8,128)(2,1)S(1)} %get-tuple-element.263), channel_id=1, source_target_pairs={{0,4},{4,8},{8,12},{12,16},{16,20},{20,24},{24,28},{1,5},{5,9},{9,... | collective-permute-start | bytes 196616 | tf_op jit(solution)/shard_map/while/body/eval_jaxpr/ppermute | solution.py:14
  148.6 7.1 %collective-permute-start = (bf16[2,64,2,128]{3,1,2,0:T(8,128)(2,1)S(1)}, bf16[2,64,2,128]{3,1,2,0:T(8,128)(2,1)S(1)}, u32[]{:S(2)}, u32[]{:S(2)}) collective-permute-start(bf16[2,64,2,128]{3,1,2,0:T(8,128)(2,1)S(1)} %get-tuple-element.263), channel_id=1, source_target_pairs={{0,4},{4,8},{8,12},{12,16},{16,20},{20,24},{24,28},{1,5},{5,9},{9,... | collective-permute-start | bytes 196616 | tf_op jit(solution)/shard_map/while/body/eval_jaxpr/ppermute | solution.py:14
  157.0 7.1 %collective-permute-start = (bf16[2,64,2,128]{3,1,2,0:T(8,128)(2,1)S(1)}, bf16[2,64,2,128]{3,1,2,0:T(8,128)(2,1)S(1)}, u32[]{:S(2)}, u32[]{:S(2)}) collective-permute-start(bf16[2,64,2,128]{3,1,2,0:T(8,128)(2,1)S(1)} %get-tuple-element.263), channel_id=1, source_target_pairs={{0,4},{4,8},{8,12},{12,16},{16,20},{20,24},{24,28},{1,5},{5,9},{9,... | collective-permute-start | bytes 196616 | tf_op jit(solution)/shard_map/while/body/eval_jaxpr/ppermute | solution.py:14
  165.5 7.1 %collective-permute-start = (bf16[2,64,2,128]{3,1,2,0:T(8,128)(2,1)S(1)}, bf16[2,64,2,128]{3,1,2,0:T(8,128)(2,1)S(1)}, u32[]{:S(2)}, u32[]{:S(2)}) collective-permute-start(bf16[2,64,2,128]{3,1,2,0:T(8,128)(2,1)S(1)} %get-tuple-element.263), channel_id=1, source_target_pairs={{0,4},{4,8},{8,12},{12,16},{16,20},{20,24},{24,28},{1,5},{5,9},{9,... | collective-permute-start | bytes 196616 | tf_op jit(solution)/shard_map/while/body/eval_jaxpr/ppermute | solution.py:14
where the time goes:
time: 190 us; the launch traced here: 189 us
  local copies, waits for them, and re-layouts  59.2 us (31%)
  waiting for transfers between devices  53.4 us (28%)
  starting transfers between devices  33.7 us (18%)
  matrix products  20.2 us (11%)
  other arithmetic  13 us (7%)
  blocking collectives  8.61 us (5%)
    ppermute x7, waiting for transfers between devices, shifted(): lax.ppermute(value, axis, [(source, source + steps) for source in range(i...  40.9 us
    scatter x1, local copies, waits for them, and re-layouts, per_device(): outgoing = outgoing.at[targets, places, head_rows].set(requested)  37.2 us
    ppermute x7, starting transfers between devices, shifted(): lax.ppermute(value, axis, [(source, source + steps) for source in range(i...  14.9 us
    all_to_all x1, waiting for transfers between devices, per_device(): lax.all_to_all(outgoing, 'seq', split_axis=0, concat_axis=0, tiled=True)  9.29 us
    all_to_all x1, blocking collectives, per_device(): lax.all_to_all(heads_out, 'kvh', split_axis=0, concat_axis=1, tiled=True)  8.61 us
    all_to_all x1, starting transfers between devices, serve_blocks(): lax.all_to_all(partial_lse, 'seq', split_axis=0, concat_axis=0, tiled=True)  6.79 us
    all_to_all x1, starting transfers between devices, per_device(): lax.all_to_all(outgoing, 'seq', split_axis=0, concat_axis=0, tiled=True)  6.2 us
    dot_general x2, matrix products, serve_blocks(): jnp.einsum('rk,kd->rd', raw_weights.astype(jnp.bfloat16), value_rows, pre...  6.11 us
  transfers between devices with their start and end apart: 10, of which 9 were waited for; matrix products, arithmetic and copies ran while one was open for 13% of the time, Pallas kernels for 0%

commit v1 on v0

v1 whole, which is shorter than its diff:
```python
import functools
import math

import jax
import jax.numpy as jnp
from jax import lax
from jax.experimental import pallas as pl
from jax.experimental.pallas import tpu as pltpu
from jax.sharding import PartitionSpec as P

BLOCK_TOKENS = 2048
MESH = pl.DeviceIdType.MESH
LOW = -1e30


def iota(shape, axis):
    return lax.broadcasted_iota(jnp.int32, shape, axis)


def dot(a, b):
    return jnp.dot(a, b, preferred_element_type=jnp.float32)


def dot_nt(a, b):
    return lax.dot_general(a, b, (((1,), (1,)), ((), ())), preferred_element_type=jnp.float32)


def one_hot(hit):
    return jnp.where(hit, 1.0, 0.0).astype(jnp.bfloat16)


def kernel(
    cfg,
    sel_ref, inv_ref, q_ref, skv_ref, cache_ref,
    out_ref,
    raw, kd, vd, qp, val, valt, qout, qin, aout, ain, lout, lin, st, m_ref, l_ref, acc, fin,
    load_sem, qs_sem, qr_sem, as_sem, ar_sem, ls_sem, lr_sem, ss_sem, sr_sem, fs_sem, fr_sem,
):
    N, KVH, KV, G, T, D, C, RP, RL, W, KEYS = cfg
    H = KV * G
    GT = G * T
    scale = 1.0 / math.sqrt(D)
    me = lax.axis_index("seq")
    mk = lax.axis_index("kvh")
    load = pltpu.make_async_copy(cache_ref, raw, load_sem)
    load.start()

    barrier = pltpu.get_barrier_semaphore()

    def greet(o, carry):
        pl.semaphore_signal(barrier, inc=1, device_id=(lax.rem(me + o, N), mk), device_id_type=MESH)
        return carry

    lax.fori_loop(1, N, greet, 0)

    def greet_kvh(o, carry):
        pl.semaphore_signal(barrier, inc=1, device_id=(me, lax.rem(mk + o, KVH)), device_id_type=MESH)
        return carry

    lax.fori_loop(1, KVH, greet_kvh, 0)

    tb = 256 // H
    r, c = iota((256, 256), 0), iota((256, 256), 1)
    order = one_hot(c == (r % tb) * H + r // tb)
    for b in range(T // tb):
        moved = dot(order, q_ref[b * 256:(b + 1) * 256, :]).astype(jnp.bfloat16)
        for h in range(H):
            qp[h // G, (h % G) * T + b * tb:(h % G) * T + (b + 1) * tb, :] = moved[h * tb:(h + 1) * tb]

    upper = one_hot(iota((T, T), 0) <= iota((T, T), 1))
    spread = one_hot(iota((T, GT), 0) == iota((T, GT), 1) % T)
    group = iota((N, GT), 1) // T
    for kv in range(KV):
        hit = inv_ref[...] == sel_ref[kv, 0:1, :]
        for k in range(1, sel_ref.shape[1]):
            hit = jnp.logical_or(hit, inv_ref[...] == sel_ref[kv, k:k + 1, :])
        rank = jnp.where(hit, dot(one_hot(hit), upper), 0.0)
        wide = dot(rank.astype(jnp.bfloat16), spread).astype(jnp.int32)
        rows = jnp.where(wide > 0, (wide - 1) * G + group, -1)
        val[kv] = rows
        padded = rows.astype(jnp.float32)
        if N < 128:
            padded = jnp.concatenate([padded, jnp.zeros((128 - N, GT), jnp.float32)], axis=0)
        valt[kv] = jnp.transpose(padded)

    pl.semaphore_wait(barrier, N - 1 + KVH - 1)

    def piece(s):
        return pltpu.make_async_remote_copy(
            src_ref=st.at[s], dst_ref=st.at[s + 1], send_sem=ss_sem.at[s], recv_sem=sr_sem.at[s + 1],
            device_id=(lax.rem(me + 1, N), mk), device_id_type=MESH,
        )

    def first_piece():
        return pltpu.make_async_remote_copy(
            src_ref=skv_ref, dst_ref=st.at[1], send_sem=ss_sem.at[0], recv_sem=sr_sem.at[1],
            device_id=(lax.rem(me + 1, N), mk), device_id_type=MESH,
        )

    def query(o, kv):
        return pltpu.make_async_remote_copy(
            src_ref=qout.at[o, kv], dst_ref=qin.at[o, kv], send_sem=qs_sem.at[o, kv],
            recv_sem=qr_sem.at[o, kv], device_id=(lax.rem(me + o, N), mk), device_id_type=MESH,
        )

    def answer(o, kv):
        return pltpu.make_async_remote_copy(
            src_ref=aout.at[o, kv], dst_ref=ain.at[o, kv], send_sem=as_sem.at[o, kv],
            recv_sem=ar_sem.at[o, kv], device_id=(lax.rem(me + N - o, N), mk), device_id_type=MESH,
        )

    def answer_lse(o):
        return pltpu.make_async_remote_copy(
            src_ref=lout.at[o], dst_ref=lin.at[o], send_sem=ls_sem.at[o],
            recv_sem=lr_sem.at[o], device_id=(lax.rem(me + N - o, N), mk), device_id_type=MESH,
        )

    if W > 1:
        @pl.when(me + 1 < N)
        def _():
            first_piece().start()

    def packed(o, kv):
        line = val[kv, pl.ds(lax.rem(me + o, N), 1), :]
        pick = one_hot(iota((RP, GT), 0) == line)
        return dot(pick, qp[kv]).astype(jnp.bfloat16)

    def send(o, carry):
        for kv in range(KV):
            qout[o, kv] = packed(o, kv)
            query(o, kv).start()
        return carry

    lax.fori_loop(1, N, send, 0)
    for kv in range(KV):
        qin[0, kv] = packed(0, kv)

    load.wait()
    split = one_hot(c == (r % (256 // KV)) * KV + r // (256 // KV))
    per = 256 // KV

    def unmix(b, carry):
        src = pl.ds(pl.multiple_of(b * 256, 256), 256)
        dst = pl.ds(pl.multiple_of(b * per, per), per)
        keys = dot(split, raw[0, src, :]).astype(jnp.bfloat16)
        values = dot(split, raw[1, src, :]).astype(jnp.bfloat16)
        for kv in range(KV):
            kd[kv, dst, :] = keys[kv * per:(kv + 1) * per]
            vd[kv, dst, :] = values[kv * per:(kv + 1) * per]
        return carry

    lax.fori_loop(0, KEYS * KV // 256, unmix, 0)

    def absorb(keys, values, causal):
        row, col = iota((GT, T * KV), 0), iota((GT, T * KV), 1)
        for kv in range(KV):
            allowed = col % KV == kv
            if causal:
                allowed = jnp.logical_and(allowed, col // KV <= row % T)
            s = jnp.where(allowed, dot_nt(qp[kv], keys) * scale, LOW)
            top = jnp.max(s, axis=1, keepdims=True)
            if causal:
                p = jnp.exp(s - top)
                m_ref[kv] = top
                l_ref[kv] = jnp.sum(p, axis=1, keepdims=True)
                acc[kv] = dot(p.astype(jnp.bfloat16), values)
            else:
                new = jnp.maximum(m_ref[kv], top)
                fade = jnp.exp(m_ref[kv] - new)
                p = jnp.exp(s - new)
                m_ref[kv] = new
                l_ref[kv] = l_ref[kv] * fade + jnp.sum(p, axis=1, keepdims=True)
                acc[kv] = acc[kv] * fade + dot(p.astype(jnp.bfloat16), values)

    absorb(skv_ref[0], skv_ref[1], True)

    def serve(o):
        for kv in range(KV):
            @pl.when(o > 0)
            def _():
                query(o, kv).wait_recv()
            s = dot_nt(qin[o, kv], kd[kv])
            top = jnp.max(s, axis=1, keepdims=True)
            p = jnp.exp((s - top) * scale)
            total = jnp.sum(p, axis=1, keepdims=True)
            res = (dot(p.astype(jnp.bfloat16), vd[kv]) / total).astype(jnp.bfloat16)
            lse = top * scale + jnp.log(total)
            flat = jnp.broadcast_to(lse, (RP, 128))
            if RL > RP:
                flat = jnp.concatenate([flat, jnp.zeros((RL - RP, 128), jnp.float32)], axis=0)
            line = jnp.transpose(flat)[0:1, :]

            @pl.when(o > 0)
            def _():
                aout[o, kv] = res
                lout[o, kv:kv + 1, :] = line
                answer(o, kv).start()

            @pl.when(o == 0)
            def _():
                ain[0, kv] = res
                lin[0, kv:kv + 1, :] = line

        @pl.when(o > 0)
        def _():
            answer_lse(o).start()

    def turn(o, carry):
        @pl.when(jnp.logical_and(o < W, jnp.logical_and(o > 0, o <= me)))
        def _():
            piece(o - 1).wait_recv()

            @pl.when(jnp.logical_and(o + 1 < W, me + 1 < N))
            def _():
                piece(o).start()

            absorb(st[o, 0], st[o, 1], False)

        serve(o)
        return carry

    lax.fori_loop(0, N, turn, 0)

    lane = iota((GT, 128), 1)
    slot = iota((GT, RL), 1)

    def merge(o, carry):
        @pl.when(o > 0)
        def _():
            answer_lse(o).wait_recv()

        dest = lax.rem(me + o, N)
        for kv in range(KV):
            @pl.when(o > 0)
            def _():
                answer(o, kv).wait_recv()
            mine = jnp.sum(jnp.where(lane == dest, valt[kv], 0.0), axis=1, keepdims=True).astype(jnp.int32)
            hit = slot == mine
            lse = jnp.sum(jnp.where(hit, lin[o, kv:kv + 1, :], 0.0), axis=1, keepdims=True)
            lse = jnp.where(mine >= 0, lse, LOW)
            got = dot(one_hot(hit[:, :RP]), ain[o, kv])
            new = jnp.maximum(m_ref[kv], lse)
            fade = jnp.exp(m_ref[kv] - new)
            w = jnp.exp(lse - new)
            m_ref[kv] = new
            l_ref[kv] = l_ref[kv] * fade + w
            acc[kv] = acc[kv] * fade + got * w
        return carry

    lax.fori_loop(0, N, merge, 0)

    for kv in range(KV):
        whole = (acc[kv] / l_ref[kv]).astype(jnp.bfloat16)
        for g in range(G):
            fin[:, (kv * G + g) * D:(kv * G + g + 1) * D] = whole[g * T:(g + 1) * T]

    TO = T // KVH
    HD = H * D
    columns = pl.ds(pl.multiple_of(mk * HD, HD), HD)

    def part(j):
        to = lax.rem(mk + j, KVH)
        return pltpu.make_async_remote_copy(
            src_ref=fin.at[pl.ds(pl.multiple_of(to * TO, TO), TO), :], dst_ref=out_ref.at[:, columns],
            send_sem=fs_sem.at[j], recv_sem=fr_sem.at[j], device_id=(me, to), device_id_type=MESH,
        )

    for j in range(1, KVH):
        part(j).start()
    own = pltpu.make_async_copy(
        fin.at[pl.ds(pl.multiple_of(mk * TO, TO), TO), :], out_ref.at[:, columns], load_sem
    )
    own.start()

    def drain(o, carry):
        for kv in range(KV):
            query(o, kv).wait_send()
            answer(o, kv).wait_send()
        answer_lse(o).wait_send()
        return carry

    lax.fori_loop(1, N, drain, 0)
    if W > 1:
        @pl.when(me + 1 < N)
        def _():
            first_piece().wait_send()

    def drain_piece(o, carry):
        @pl.when(jnp.logical_and(o <= me, me + 1 < N))
        def _():
            piece(o).wait_send()
        return carry

    lax.fori_loop(1, W - 1, drain_piece, 0)
    own.wait()
    for j in range(1, KVH):
        part(j).wait()


def per_device(queries, stretch_kv, cache_kv, selection, block_owner):
    T, H, D = queries.shape
    KV = stretch_kv.shape[2]
    G = H // KV
    top = selection.shape[2]
    N = lax.axis_size("seq")
    KVH = lax.axis_size("kvh")
    C = max(2, top * T // N + 1)
    RP = -(-C * G // 16) * 16
    RL = -(-RP // 128) * 128
    W = min(BLOCK_TOKENS // T, N)
    KEYS = cache_kv.shape[2]
    cfg = (N, KVH, KV, G, T, D, C, RP, RL, W, KEYS)
    places = jnp.arange(N, dtype=jnp.int32)
    inverse = jnp.sum(
        jnp.where(block_owner[None, :] == places[:, None], places[None, :], 0), axis=1, keepdims=True
    )
    bf, f32 = jnp.bfloat16, jnp.float32
    vm = pl.BlockSpec(memory_space=pltpu.VMEM)
    dma = pltpu.SemaphoreType.DMA
    return pl.pallas_call(
        functools.partial(kernel, cfg),
        out_shape=jax.ShapeDtypeStruct((T // KVH, KVH * H * D), bf),
        in_specs=[vm, vm, vm, vm, pl.BlockSpec(memory_space=pl.ANY)],
        out_specs=vm,
        scratch_shapes=[
            pltpu.VMEM((2, KEYS * KV, D), bf),
            pltpu.VMEM((KV, KEYS, D), bf),
            pltpu.VMEM((KV, KEYS, D), bf),
            pltpu.VMEM((KV, G * T, D), bf),
            pltpu.VMEM((KV, N, G * T), jnp.int32),
            pltpu.VMEM((KV, G * T, 128), f32),
            pltpu.VMEM((N, KV, RP, D), bf),
            pltpu.VMEM((N, KV, RP, D), bf),
            pltpu.VMEM((N, KV, RP, D), bf),
            pltpu.VMEM((N, KV, RP, D), bf),
            pltpu.VMEM((N, 8, RL), f32),
            pltpu.VMEM((N, 8, RL), f32),
            pltpu.VMEM((W, 2, T * KV, D), bf),
            pltpu.VMEM((KV, G * T, 1), f32),
            pltpu.VMEM((KV, G * T, 1), f32),
            pltpu.VMEM((KV, G * T, D), f32),
            pltpu.VMEM((T, H * D), bf),
            dma, dma((N, KV)), dma((N, KV)), dma((N, KV)), dma((N, KV)), dma((N,)), dma((N,)),
            dma((W,)), dma((W,)), dma((KVH,)), dma((KVH,)),
        ],
        compiler_params=pltpu.CompilerParams(
            collective_id=0, has_side_effects=True, vmem_limit_bytes=56 * 1024 * 1024
        ),
        cost_estimate=pl.CostEstimate(
            flops=4 * N * RP * KV * KEYS * D, bytes_accessed=4 * KEYS * KV * D, transcendentals=N * RP * KV * KEYS
        ),
    )(
        jnp.swapaxes(selection, 1, 2),
        inverse,
        queries.reshape(T * H, D),
        stretch_kv.reshape(2, T * KV, D),
        cache_kv.reshape(2, KEYS * KV, D),
    )


def solution(mesh):
    placed = (
        P("seq", "kvh", None),
        P(None, "seq", "kvh", None),
        P(None, "seq", None, "kvh", None),
        P("kvh", "seq", None),
        P(),
    )
    return jax.shard_map(
        per_device, mesh=mesh, in_specs=placed, out_specs=P(("seq", "kvh"), None), check_vma=False
    )
```

time: 190 us -> 77.9 us (0.41)
  the two profiles are of different devices: /device:TPU:16 before, /device:TPU:1 now
where the time goes in v1:
time: 77.9 us; the launch traced here: 77.7 us
  Pallas kernels  73.3 us (94%)
  local copies, waits for them, and re-layouts  3.62 us (5%)
    pallas_call x1, Pallas kernels, per_device(): pl.pallas_call(functools.partial(kernel, cfg), out_shape=jax.ShapeDtypeSt...  73.3 us
    unnamed x2, local copies, waits for them, and re-layouts  2.95 us

profile of v1, /device:TPU:1, one launch (start us, length us, event | category | flops | bytes accessed | tf_op | source)
XLA Modules:
  0.0 77.7 jit_solution(12087666801469268924)
XLA Ops:
  0.0 0.8 select_reduce_fusion
  0.8 0.7 copy.9.inv_ref
  1.4 1.3 %copy.11 = s32[2,64,3]{1,2,0:T(4,128)} copy(s32[2,64,3]{1,0,2:T(2,128)} %param.8) | data formatting | bytes 3072 | tf_op args[3]
  2.7 73.3 %shard_map.55 = bf16[16,8192]{1,0:T(8,128)(2,1)} custom-call(s32[2,3,64]{2,1,0:T(4,128)} %bitcast.7, s32[8,1]{1,0:T(8,128)} %copy.9.inv_ref, bf16[1024,128]{1,0:T(8,128)(2,1)} %bitcast.10, bf16[2,128,128]{2,1,0:T(8,128)(2,1)} %bitcast.11, bf16[2,4096,128]{2,1,0:T(8,128)(2,1)} %bitcast.9), custom_call_target="tpu_custom_call" | custom-call | flops 3489660928 | bytes 2097152 | tf_op jit(solution)/shard_map/pallas_call | solution.py:320
  76.1 1.7 %copy.13 = bf16[16,8192]{1,0:T(8,128)(2,1)} copy(bf16[16,8192]{1,0:T(8,128)(2,1)} %shard_map.55) | data formatting | bytes 524288

commit v2 on v1

--- a/solution.py
+++ b/solution.py
@@ -11,6 +11,7 @@
 BLOCK_TOKENS = 2048
 MESH = pl.DeviceIdType.MESH
 LOW = -1e30
+LOG2E = math.log2(math.e)
 
 
 def iota(shape, axis):
@@ -31,9 +32,9 @@
 
 def kernel(
     cfg,
-    sel_ref, inv_ref, q_ref, skv_ref, cache_ref,
+    sel_ref, owner_ref, q_ref, skv_ref, cache_ref,
     out_ref,
-    raw, kd, vd, qp, val, valt, qout, qin, aout, ain, lout, lin, st, m_ref, l_ref, acc, fin,
+    raw, kd, vd, qp, val, valt, qout, qin, aout, ain, lout, lin, st, sk, sv, m_ref, l_ref, acc, fin,
     load_sem, qs_sem, qr_sem, as_sem, ar_sem, ls_sem, lr_sem, ss_sem, sr_sem, fs_sem, fr_sem,
 ):
     N, KVH, KV, G, T, D, C, RP, RL, W, KEYS = cfg
@@ -68,13 +69,16 @@
             qp[h // G, (h % G) * T + b * tb:(h % G) * T + (b + 1) * tb, :] = moved[h * tb:(h + 1) * tb]
 
     upper = one_hot(iota((T, T), 0) <= iota((T, T), 1))
+    same = one_hot(iota((T, T), 0) == iota((T, T), 1))
     spread = one_hot(iota((T, GT), 0) == iota((T, GT), 1) % T)
     group = iota((N, GT), 1) // T
+    owns = one_hot(iota((N, N), 0) == owner_ref[...])
     for kv in range(KV):
-        hit = inv_ref[...] == sel_ref[kv, 0:1, :]
-        for k in range(1, sel_ref.shape[1]):
-            hit = jnp.logical_or(hit, inv_ref[...] == sel_ref[kv, k:k + 1, :])
-        rank = jnp.where(hit, dot(one_hot(hit), upper), 0.0)
+        named = iota((T, N), 1) == sel_ref[kv, :, 0:1]
+        for k in range(1, sel_ref.shape[2]):
+            named = jnp.logical_or(named, iota((T, N), 1) == sel_ref[kv, :, k:k + 1])
+        named = dot_nt(owns, one_hot(named)).astype(jnp.bfloat16)
+        rank = dot(named, upper) * dot(named, same)
         wide = dot(rank.astype(jnp.bfloat16), spread).astype(jnp.int32)
         rows = jnp.where(wide > 0, (wide - 1) * G + group, -1)
         val[kv] = rows
@@ -97,16 +101,16 @@
             device_id=(lax.rem(me + 1, N), mk), device_id_type=MESH,
         )
 
-    def query(o, kv):
-        return pltpu.make_async_remote_copy(
-            src_ref=qout.at[o, kv], dst_ref=qin.at[o, kv], send_sem=qs_sem.at[o, kv],
-            recv_sem=qr_sem.at[o, kv], device_id=(lax.rem(me + o, N), mk), device_id_type=MESH,
-        )
-
-    def answer(o, kv):
-        return pltpu.make_async_remote_copy(
-            src_ref=aout.at[o, kv], dst_ref=ain.at[o, kv], send_sem=as_sem.at[o, kv],
-            recv_sem=ar_sem.at[o, kv], device_id=(lax.rem(me + N - o, N), mk), device_id_type=MESH,
+    def query(o):
+        return pltpu.make_async_remote_copy(
+            src_ref=qout.at[o], dst_ref=qin.at[o], send_sem=qs_sem.at[o],
+            recv_sem=qr_sem.at[o], device_id=(lax.rem(me + o, N), mk), device_id_type=MESH,
+        )
+
+    def answer(o):
+        return pltpu.make_async_remote_copy(
+            src_ref=aout.at[o], dst_ref=ain.at[o], send_sem=as_sem.at[o],
+            recv_sem=ar_sem.at[o], device_id=(lax.rem(me + N - o, N), mk), device_id_type=MESH,
         )
 
     def answer_lse(o):
@@ -128,7 +132,7 @@
     def send(o, carry):
         for kv in range(KV):
             qout[o, kv] = packed(o, kv)
-            query(o, kv).start()
+        query(o).start()
         return carry
 
     lax.fori_loop(1, N, send, 0)
@@ -146,67 +150,35 @@
         values = dot(split, raw[1, src, :]).astype(jnp.bfloat16)
         for kv in range(KV):
             kd[kv, dst, :] = keys[kv * per:(kv + 1) * per]
-            vd[kv, dst, :] = values[kv * per:(kv + 1) * per]
+            vd[kv, dst, 0:D] = values[kv * per:(kv + 1) * per]
+            vd[kv, dst, D:2 * D] = jnp.ones((per, D), jnp.bfloat16)
         return carry
 
     lax.fori_loop(0, KEYS * KV // 256, unmix, 0)
 
-    def absorb(keys, values, causal):
-        row, col = iota((GT, T * KV), 0), iota((GT, T * KV), 1)
-        for kv in range(KV):
-            allowed = col % KV == kv
-            if causal:
-                allowed = jnp.logical_and(allowed, col // KV <= row % T)
-            s = jnp.where(allowed, dot_nt(qp[kv], keys) * scale, LOW)
-            top = jnp.max(s, axis=1, keepdims=True)
-            if causal:
-                p = jnp.exp(s - top)
-                m_ref[kv] = top
-                l_ref[kv] = jnp.sum(p, axis=1, keepdims=True)
-                acc[kv] = dot(p.astype(jnp.bfloat16), values)
-            else:
-                new = jnp.maximum(m_ref[kv], top)
-                fade = jnp.exp(m_ref[kv] - new)
-                p = jnp.exp(s - new)
-                m_ref[kv] = new
-                l_ref[kv] = l_ref[kv] * fade + jnp.sum(p, axis=1, keepdims=True)
-                acc[kv] = acc[kv] * fade + dot(p.astype(jnp.bfloat16), values)
-
-    absorb(skv_ref[0], skv_ref[1], True)
-
-    def serve(o):
-        for kv in range(KV):
-            @pl.when(o > 0)
-            def _():
-                query(o, kv).wait_recv()
+    def serve(o, answers, lines):
+        for kv in range(KV):
             s = dot_nt(qin[o, kv], kd[kv])
             top = jnp.max(s, axis=1, keepdims=True)
-            p = jnp.exp((s - top) * scale)
-            total = jnp.sum(p, axis=1, keepdims=True)
-            res = (dot(p.astype(jnp.bfloat16), vd[kv]) / total).astype(jnp.bfloat16)
-            lse = top * scale + jnp.log(total)
-            flat = jnp.broadcast_to(lse, (RP, 128))
+            p = jnp.exp2((s - top) * (scale * LOG2E)).astype(jnp.bfloat16)
+            res = dot(p, vd[kv])
+            total = res[:, D:2 * D]
+            answers[o, kv] = (res[:, 0:D] / total).astype(jnp.bfloat16)
+            flat = top * scale + jnp.log(total)
             if RL > RP:
-                flat = jnp.concatenate([flat, jnp.zeros((RL - RP, 128), jnp.float32)], axis=0)
-            line = jnp.transpose(flat)[0:1, :]
-
-            @pl.when(o > 0)
-            def _():
-                aout[o, kv] = res
-                lout[o, kv:kv + 1, :] = line
-                answer(o, kv).start()
-
-            @pl.when(o == 0)
-            def _():
-                ain[0, kv] = res
-                lin[0, kv:kv + 1, :] = line
-
-        @pl.when(o > 0)
-        def _():
-            answer_lse(o).start()
+                flat = jnp.concatenate([flat, jnp.zeros((RL - RP, D), jnp.float32)], axis=0)
+            lines[o, kv:kv + 1, :] = jnp.transpose(flat)[0:1, :]
+
+    def blank(o, carry):
+        st[o] = jnp.zeros((2, T * KV, D), jnp.bfloat16)
+        return carry
+
+    st[0] = skv_ref[...]
+    lax.fori_loop(me + 1, W, blank, 0)
+    serve(0, ain, lin)
 
     def turn(o, carry):
-        @pl.when(jnp.logical_and(o < W, jnp.logical_and(o > 0, o <= me)))
+        @pl.when(jnp.logical_and(o < W, o <= me))
         def _():
             piece(o - 1).wait_recv()
 
@@ -214,12 +186,35 @@
             def _():
                 piece(o).start()
 
-            absorb(st[o, 0], st[o, 1], False)
-
-        serve(o)
-        return carry
-
-    lax.fori_loop(0, N, turn, 0)
+        query(o).wait_recv()
+        serve(o, aout, lout)
+        answer(o).start()
+        answer_lse(o).start()
+        return carry
+
+    lax.fori_loop(1, N, turn, 0)
+
+    pt = 256 // (T * KV)
+    c2 = iota((256, 256), 1)
+    r2 = iota((256, 256), 0)
+    apart = one_hot(c2 == (r2 % (pt * T)) * KV + r2 // (pt * T))
+    for b in range(W // pt):
+        keys = dot(apart, st[b * pt:(b + 1) * pt, 0].reshape(256, D)).astype(jnp.bfloat16)
+        values = dot(apart, st[b * pt:(b + 1) * pt, 1].reshape(256, D)).astype(jnp.bfloat16)
+        for kv in range(KV):
+            sk[kv, b * pt * T:(b + 1) * pt * T, :] = keys[kv * pt * T:(kv + 1) * pt * T]
+            sv[kv, b * pt * T:(b + 1) * pt * T, 0:D] = values[kv * pt * T:(kv + 1) * pt * T]
+            sv[kv, b * pt * T:(b + 1) * pt * T, D:2 * D] = jnp.ones((pt * T, D), jnp.bfloat16)
+    row, col = iota((GT, W * T), 0), iota((GT, W * T), 1)
+    allowed = jnp.logical_and(col < (me + 1) * T, col <= row % T + jnp.where(col < T, 0, W * T))
+    for kv in range(KV):
+        s = jnp.where(allowed, dot_nt(qp[kv], sk[kv]), LOW)
+        top = jnp.max(s, axis=1, keepdims=True)
+        p = jnp.exp2((s - top) * (scale * LOG2E)).astype(jnp.bfloat16)
+        res = dot(p, sv[kv])
+        m_ref[kv] = top * scale
+        l_ref[kv] = res[:, D:D + 1]
+        acc[kv] = res[:, 0:D]
 
     lane = iota((GT, 128), 1)
     slot = iota((GT, RL), 1)
@@ -227,13 +222,11 @@
     def merge(o, carry):
         @pl.when(o > 0)
         def _():
+            answer(o).wait_recv()
             answer_lse(o).wait_recv()
 
         dest = lax.rem(me + o, N)
         for kv in range(KV):
-            @pl.when(o > 0)
-            def _():
-                answer(o, kv).wait_recv()
             mine = jnp.sum(jnp.where(lane == dest, valt[kv], 0.0), axis=1, keepdims=True).astype(jnp.int32)
             hit = slot == mine
             lse = jnp.sum(jnp.where(hit, lin[o, kv:kv + 1, :], 0.0), axis=1, keepdims=True)
@@ -273,9 +266,8 @@
     own.start()
 
     def drain(o, carry):
-        for kv in range(KV):
-            query(o, kv).wait_send()
-            answer(o, kv).wait_send()
+        query(o).wait_send()
+        answer(o).wait_send()
         answer_lse(o).wait_send()
         return carry
 
@@ -310,10 +302,6 @@
     W = min(BLOCK_TOKENS // T, N)
     KEYS = cache_kv.shape[2]
     cfg = (N, KVH, KV, G, T, D, C, RP, RL, W, KEYS)
-    places = jnp.arange(N, dtype=jnp.int32)
-    inverse = jnp.sum(
-        jnp.where(block_owner[None, :] == places[:, None], places[None, :], 0), axis=1, keepdims=True
-    )
     bf, f32 = jnp.bfloat16, jnp.float32
     vm = pl.BlockSpec(memory_space=pltpu.VMEM)
     dma = pltpu.SemaphoreType.DMA
@@ -325,7 +313,7 @@
         scratch_shapes=[
             pltpu.VMEM((2, KEYS * KV, D), bf),
             pltpu.VMEM((KV, KEYS, D), bf),
-            pltpu.VMEM((KV, KEYS, D), bf),
+            pltpu.VMEM((KV, KEYS, 2 * D), bf),
             pltpu.VMEM((KV, G * T, D), bf),
             pltpu.VMEM((KV, N, G * T), jnp.int32),
             pltpu.VMEM((KV, G * T, 128), f32),
@@ -336,11 +324,13 @@
             pltpu.VMEM((N, 8, RL), f32),
             pltpu.VMEM((N, 8, RL), f32),
             pltpu.VMEM((W, 2, T * KV, D), bf),
+            pltpu.VMEM((KV, W * T, D), bf),
+            pltpu.VMEM((KV, W * T, 2 * D), bf),
             pltpu.VMEM((KV, G * T, 1), f32),
             pltpu.VMEM((KV, G * T, 1), f32),
             pltpu.VMEM((KV, G * T, D), f32),
             pltpu.VMEM((T, H * D), bf),
-            dma, dma((N, KV)), dma((N, KV)), dma((N, KV)), dma((N, KV)), dma((N,)), dma((N,)),
+            dma, dma((N,)), dma((N,)), dma((N,)), dma((N,)), dma((N,)), dma((N,)),
             dma((W,)), dma((W,)), dma((KVH,)), dma((KVH,)),
         ],
         compiler_params=pltpu.CompilerParams(
@@ -350,8 +340,8 @@
             flops=4 * N * RP * KV * KEYS * D, bytes_accessed=4 * KEYS * KV * D, transcendentals=N * RP * KV * KEYS
         ),
     )(
-        jnp.swapaxes(selection, 1, 2),
-        inverse,
+        selection,
+        block_owner.reshape(1, N),
         queries.reshape(T * H, D),
         stretch_kv.reshape(2, T * KV, D),
         cache_kv.reshape(2, KEYS * KV, D),

time: 77.9 us -> 73.3 us (0.941)
  Pallas kernels: 73.3 us -> 70 us
    pallas_call x1, Pallas kernels: 73.3 us -> 70 us  [per_device(): pl.pallas_call(functools.partial(kernel, cfg), out_shape=jax.ShapeDtypeSt...]
where the time goes in v2:
time: 73.3 us; the launch traced here: 73.1 us
  Pallas kernels  70 us (95%)
  local copies, waits for them, and re-layouts  3.09 us (4%)
    pallas_call x1, Pallas kernels, per_device(): pl.pallas_call(functools.partial(kernel, cfg), out_shape=jax.ShapeDtypeSt...  70 us
    unnamed x2, local copies, waits for them, and re-layouts  3.09 us

profile of v2, /device:TPU:1, one launch (start us, length us, event | category | flops | bytes accessed | tf_op | source)
XLA Modules:
  0.0 73.1 jit_solution(8859529680614714260)
XLA Ops:
  0.0 1.4 %copy.6.sel_ref = s32[2,64,3]{2,1,0:T(8,128)} copy(s32[2,64,3]{1,0,2:T(2,128)} %param.8) | data formatting | bytes 3072 | tf_op args[3]
  1.4 70.0 %shard_map.55 = bf16[16,8192]{1,0:T(8,128)(2,1)} custom-call(s32[2,64,3]{2,1,0:T(8,128)} %copy.6.sel_ref, s32[1,8]{1,0:T(1,128)} %bitcast.7, bf16[1024,128]{1,0:T(8,128)(2,1)} %bitcast.5, bf16[2,128,128]{2,1,0:T(8,128)(2,1)} %bitcast.6, bf16[2,4096,128]{2,1,0:T(8,128)(2,1)} %bitcast.4), custom_call_target="tpu_custom_call" | custom-call | flops 3489660928 | bytes 2097152 | tf_op jit(solution)/shard_map/pallas_call | solution.py:308
  71.4 1.7 %copy.8 = bf16[16,8192]{1,0:T(8,128)(2,1)} copy(bf16[16,8192]{1,0:T(8,128)(2,1)} %shard_map.55) | data formatting | bytes 524288

commit v3 on v2

--- a/solution.py
+++ b/solution.py
@@ -85,53 +85,57 @@
         padded = rows.astype(jnp.float32)
         if N < 128:
             padded = jnp.concatenate([padded, jnp.zeros((128 - N, GT), jnp.float32)], axis=0)
-        valt[kv] = jnp.transpose(padded)
-
-    pl.semaphore_wait(barrier, N - 1 + KVH - 1)
-
-    def piece(s):
-        return pltpu.make_async_remote_copy(
-            src_ref=st.at[s], dst_ref=st.at[s + 1], send_sem=ss_sem.at[s], recv_sem=sr_sem.at[s + 1],
-            device_id=(lax.rem(me + 1, N), mk), device_id_type=MESH,
-        )
-
-    def first_piece():
-        return pltpu.make_async_remote_copy(
-            src_ref=skv_ref, dst_ref=st.at[1], send_sem=ss_sem.at[0], recv_sem=sr_sem.at[1],
-            device_id=(lax.rem(me + 1, N), mk), device_id_type=MESH,
-        )
-
-    def query(o):
-        return pltpu.make_async_remote_copy(
-            src_ref=qout.at[o], dst_ref=qin.at[o], send_sem=qs_sem.at[o],
-            recv_sem=qr_sem.at[o], device_id=(lax.rem(me + o, N), mk), device_id_type=MESH,
-        )
-
-    def answer(o):
-        return pltpu.make_async_remote_copy(
-            src_ref=aout.at[o], dst_ref=ain.at[o], send_sem=as_sem.at[o],
-            recv_sem=ar_sem.at[o], device_id=(lax.rem(me + N - o, N), mk), device_id_type=MESH,
-        )
-
-    def answer_lse(o):
-        return pltpu.make_async_remote_copy(
-            src_ref=lout.at[o], dst_ref=lin.at[o], send_sem=ls_sem.at[o],
-            recv_sem=lr_sem.at[o], device_id=(lax.rem(me + N - o, N), mk), device_id_type=MESH,
-        )
-
-    if W > 1:
-        @pl.when(me + 1 < N)
-        def _():
-            first_piece().start()
+        valt[kv] = jnp.transpose(padded).astype(jnp.bfloat16)
 
     def packed(o, kv):
         line = val[kv, pl.ds(lax.rem(me + o, N), 1), :]
         pick = one_hot(iota((RP, GT), 0) == line)
         return dot(pick, qp[kv]).astype(jnp.bfloat16)
 
+    def pack(o, carry):
+        for kv in range(KV):
+            qout[o, kv] = packed(o, kv)
+        return carry
+
+    lax.fori_loop(1, N, pack, 0)
+    pl.semaphore_wait(barrier, N - 1 + KVH - 1)
+
+    def piece(s):
+        return pltpu.make_async_remote_copy(
+            src_ref=st.at[s], dst_ref=st.at[s + 1], send_sem=ss_sem.at[s], recv_sem=sr_sem.at[s + 1],
+            device_id=(lax.rem(me + 1, N), mk), device_id_type=MESH,
+        )
+
+    def first_piece():
+        return pltpu.make_async_remote_copy(
+            src_ref=skv_ref, dst_ref=st.at[1], send_sem=ss_sem.at[0], recv_sem=sr_sem.at[1],
+            device_id=(lax.rem(me + 1, N), mk), device_id_type=MESH,
+        )
+
+    def query(o):
+        return pltpu.make_async_remote_copy(
+            src_ref=qout.at[o], dst_ref=qin.at[o], send_sem=qs_sem.at[o],
+            recv_sem=qr_sem.at[o], device_id=(lax.rem(me + o, N), mk), device_id_type=MESH,
+        )
+
+    def answer(o):
+        return pltpu.make_async_remote_copy(
+            src_ref=aout.at[o], dst_ref=ain.at[o], send_sem=as_sem.at[o],
+            recv_sem=ar_sem.at[o], device_id=(lax.rem(me + N - o, N), mk), device_id_type=MESH,
+        )
+
+    def answer_lse(o):
+        return pltpu.make_async_remote_copy(
+            src_ref=lout.at[o], dst_ref=lin.at[o], send_sem=ls_sem.at[o],
+            recv_sem=lr_sem.at[o], device_id=(lax.rem(me + N - o, N), mk), device_id_type=MESH,
+        )
+
+    if W > 1:
+        @pl.when(me + 1 < N)
+        def _():
+            first_piece().start()
+
     def send(o, carry):
-        for kv in range(KV):
-            qout[o, kv] = packed(o, kv)
         query(o).start()
         return carry
 
@@ -149,25 +153,29 @@
         keys = dot(split, raw[0, src, :]).astype(jnp.bfloat16)
         values = dot(split, raw[1, src, :]).astype(jnp.bfloat16)
         for kv in range(KV):
-            kd[kv, dst, :] = keys[kv * per:(kv + 1) * per]
+            kd[kv, :, dst] = jnp.transpose(keys[kv * per:(kv + 1) * per])
             vd[kv, dst, 0:D] = values[kv * per:(kv + 1) * per]
             vd[kv, dst, D:2 * D] = jnp.ones((per, D), jnp.bfloat16)
         return carry
 
     lax.fori_loop(0, KEYS * KV // 256, unmix, 0)
 
-    def serve(o, answers, lines):
-        for kv in range(KV):
-            s = dot_nt(qin[o, kv], kd[kv])
+    def serve(first, count, answers, lines):
+        for kv in range(KV):
+            rows = [qin[first + i, kv] for i in range(count)]
+            s = dot(rows[0] if count == 1 else jnp.concatenate(rows, axis=0), kd[kv])
             top = jnp.max(s, axis=1, keepdims=True)
             p = jnp.exp2((s - top) * (scale * LOG2E)).astype(jnp.bfloat16)
             res = dot(p, vd[kv])
             total = res[:, D:2 * D]
-            answers[o, kv] = (res[:, 0:D] / total).astype(jnp.bfloat16)
-            flat = top * scale + jnp.log(total)
-            if RL > RP:
-                flat = jnp.concatenate([flat, jnp.zeros((RL - RP, D), jnp.float32)], axis=0)
-            lines[o, kv:kv + 1, :] = jnp.transpose(flat)[0:1, :]
+            out = (res[:, 0:D] / total).astype(jnp.bfloat16)
+            lse = top * scale + jnp.log(total)
+            for i in range(count):
+                answers[first + i, kv] = out[i * RP:(i + 1) * RP]
+                flat = lse[i * RP:(i + 1) * RP]
+                if RL > RP:
+                    flat = jnp.concatenate([flat, jnp.zeros((RL - RP, D), jnp.float32)], axis=0)
+                lines[first + i, kv:kv + 1, :] = jnp.transpose(flat)[0:1, :]
 
     def blank(o, carry):
         st[o] = jnp.zeros((2, T * KV, D), jnp.bfloat16)
@@ -175,9 +183,9 @@
 
     st[0] = skv_ref[...]
     lax.fori_loop(me + 1, W, blank, 0)
-    serve(0, ain, lin)
-
-    def turn(o, carry):
+    serve(0, 1, ain, lin)
+
+    def pass_on(o):
         @pl.when(jnp.logical_and(o < W, o <= me))
         def _():
             piece(o - 1).wait_recv()
@@ -186,13 +194,23 @@
             def _():
                 piece(o).start()
 
-        query(o).wait_recv()
-        serve(o, aout, lout)
-        answer(o).start()
-        answer_lse(o).start()
-        return carry
-
-    lax.fori_loop(1, N, turn, 0)
+    def turn(first, count):
+        for i in range(count):
+            pass_on(first + i)
+        for i in range(count):
+            query(first + i).wait_recv()
+        serve(first, count, aout, lout)
+        for i in range(count):
+            answer(first + i).start()
+            answer_lse(first + i).start()
+
+    def two(i, carry):
+        turn(1 + 2 * i, 2)
+        return carry
+
+    lax.fori_loop(0, (N - 1) // 2, two, 0)
+    if (N - 1) % 2:
+        turn(N - 1, 1)
 
     pt = 256 // (T * KV)
     c2 = iota((256, 256), 1)
@@ -212,12 +230,17 @@
         top = jnp.max(s, axis=1, keepdims=True)
         p = jnp.exp2((s - top) * (scale * LOG2E)).astype(jnp.bfloat16)
         res = dot(p, sv[kv])
-        m_ref[kv] = top * scale
-        l_ref[kv] = res[:, D:D + 1]
+        m_ref[kv] = jnp.broadcast_to(top * scale, (GT, D))
+        l_ref[kv] = res[:, D:2 * D]
         acc[kv] = res[:, 0:D]
 
-    lane = iota((GT, 128), 1)
-    slot = iota((GT, RL), 1)
+    slot = iota((GT, RL), 1).astype(jnp.float32)
+
+    def thirds(x):
+        high = x.astype(jnp.bfloat16)
+        x = x - high.astype(jnp.float32)
+        middle = x.astype(jnp.bfloat16)
+        return high, middle, (x - middle.astype(jnp.float32)).astype(jnp.bfloat16)
 
     def merge(o, carry):
         @pl.when(o > 0)
@@ -226,12 +249,17 @@
             answer_lse(o).wait_recv()
 
         dest = lax.rem(me + o, N)
-        for kv in range(KV):
-            mine = jnp.sum(jnp.where(lane == dest, valt[kv], 0.0), axis=1, keepdims=True).astype(jnp.int32)
-            hit = slot == mine
-            lse = jnp.sum(jnp.where(hit, lin[o, kv:kv + 1, :], 0.0), axis=1, keepdims=True)
-            lse = jnp.where(mine >= 0, lse, LOW)
-            got = dot(one_hot(hit[:, :RP]), ain[o, kv])
+        column = one_hot(iota((128, RL), 0) == dest)
+        for kv in range(KV):
+            mine = dot(valt[kv], column)
+            hit = one_hot(mine == slot)[:, :RP]
+            lines = jnp.broadcast_to(lin[o, kv:kv + 1, :], (D, RL))
+            high, middle, low = thirds(jnp.transpose(lines)[:RP])
+            got = dot(hit, jnp.concatenate([ain[o, kv], high], axis=1))
+            rest = dot(hit, jnp.concatenate([middle, low], axis=1))
+            lse = got[:, D:2 * D] + rest[:, 0:D] + rest[:, D:2 * D]
+            lse = jnp.where(mine[:, 0:D] >= 0, lse, LOW)
+            got = got[:, 0:D]
             new = jnp.maximum(m_ref[kv], lse)
             fade = jnp.exp(m_ref[kv] - new)
             w = jnp.exp(lse - new)
@@ -312,11 +340,11 @@
         out_specs=vm,
         scratch_shapes=[
             pltpu.VMEM((2, KEYS * KV, D), bf),
-            pltpu.VMEM((KV, KEYS, D), bf),
+            pltpu.VMEM((KV, D, KEYS), bf),
             pltpu.VMEM((KV, KEYS, 2 * D), bf),
             pltpu.VMEM((KV, G * T, D), bf),
             pltpu.VMEM((KV, N, G * T), jnp.int32),
-            pltpu.VMEM((KV, G * T, 128), f32),
+            pltpu.VMEM((KV, G * T, 128), bf),
             pltpu.VMEM((N, KV, RP, D), bf),
             pltpu.VMEM((N, KV, RP, D), bf),
             pltpu.VMEM((N, KV, RP, D), bf),
@@ -326,8 +354,8 @@
             pltpu.VMEM((W, 2, T * KV, D), bf),
             pltpu.VMEM((KV, W * T, D), bf),
             pltpu.VMEM((KV, W * T, 2 * D), bf),
-            pltpu.VMEM((KV, G * T, 1), f32),
-            pltpu.VMEM((KV, G * T, 1), f32),
+            pltpu.VMEM((KV, G * T, D), f32),
+            pltpu.VMEM((KV, G * T, D), f32),
             pltpu.VMEM((KV, G * T, D), f32),
             pltpu.VMEM((T, H * D), bf),
             dma, dma((N,)), dma((N,)), dma((N,)), dma((N,)), dma((N,)), dma((N,)),

time: 73.3 us -> 77.5 us (1.057)
  Pallas kernels: 70 us -> 74.2 us
    pallas_call x1, Pallas kernels: 70 us -> 74.2 us  [per_device(): pl.pallas_call(functools.partial(kernel, cfg), out_shape=jax.ShapeDtypeSt...]
where the time goes in v3:
time: 77.5 us; the launch traced here: 77.3 us
  Pallas kernels  74.2 us (96%)
  local copies, waits for them, and re-layouts  3.09 us (4%)
    pallas_call x1, Pallas kernels, per_device(): pl.pallas_call(functools.partial(kernel, cfg), out_shape=jax.ShapeDtypeSt...  74.2 us
    unnamed x2, local copies, waits for them, and re-layouts  3.09 us

profile of v3, /device:TPU:1, one launch (start us, length us, event | category | flops | bytes accessed | tf_op | source)
XLA Modules:
  0.0 77.3 jit_solution(11507096112950565234)
XLA Ops:
  0.0 1.4 %copy.6.sel_ref = s32[2,64,3]{2,1,0:T(8,128)} copy(s32[2,64,3]{1,0,2:T(2,128)} %param.8) | data formatting | bytes 3072 | tf_op args[3]
  1.4 74.2 %shard_map.55 = bf16[16,8192]{1,0:T(8,128)(2,1)} custom-call(s32[2,64,3]{2,1,0:T(8,128)} %copy.6.sel_ref, s32[1,8]{1,0:T(1,128)} %bitcast.7, bf16[1024,128]{1,0:T(8,128)(2,1)} %bitcast.5, bf16[2,128,128]{2,1,0:T(8,128)(2,1)} %bitcast.6, bf16[2,4096,128]{2,1,0:T(8,128)(2,1)} %bitcast.4), custom_call_target="tpu_custom_call" | custom-call | flops 3489660928 | bytes 2097152 | tf_op jit(solution)/shard_map/pallas_call | solution.py:336
  75.7 1.7 %copy.8 = bf16[16,8192]{1,0:T(8,128)(2,1)} copy(bf16[16,8192]{1,0:T(8,128)(2,1)} %shard_map.55) | data formatting | bytes 524288

commit v4 on v2

--- a/solution.py
+++ b/solution.py
@@ -35,7 +35,7 @@
     sel_ref, owner_ref, q_ref, skv_ref, cache_ref,
     out_ref,
     raw, kd, vd, qp, val, valt, qout, qin, aout, ain, lout, lin, st, sk, sv, m_ref, l_ref, acc, fin,
-    load_sem, qs_sem, qr_sem, as_sem, ar_sem, ls_sem, lr_sem, ss_sem, sr_sem, fs_sem, fr_sem,
+    load_sem, qs_sem, qr_sem, as_sem, ar_sem, ls_sem, lr_sem, ss_sem, ps_sem, sr_sem, fs_sem, fr_sem,
 ):
     N, KVH, KV, G, T, D, C, RP, RL, W, KEYS = cfg
     H = KV * G
@@ -89,17 +89,32 @@
 
     pl.semaphore_wait(barrier, N - 1 + KVH - 1)
 
-    def piece(s):
-        return pltpu.make_async_remote_copy(
-            src_ref=st.at[s], dst_ref=st.at[s + 1], send_sem=ss_sem.at[s], recv_sem=sr_sem.at[s + 1],
-            device_id=(lax.rem(me + 1, N), mk), device_id_type=MESH,
-        )
-
-    def first_piece():
-        return pltpu.make_async_remote_copy(
-            src_ref=skv_ref, dst_ref=st.at[1], send_sem=ss_sem.at[0], recv_sem=sr_sem.at[1],
-            device_id=(lax.rem(me + 1, N), mk), device_id_type=MESH,
-        )
+    odd = lax.rem(me, 2)
+
+    def chain(s):
+        return pltpu.make_async_remote_copy(
+            src_ref=st.at[s], dst_ref=st.at[s + 2], send_sem=ss_sem.at[s], recv_sem=sr_sem.at[s + 2],
+            device_id=(lax.rem(me + 2, N), mk), device_id_type=MESH,
+        )
+
+    def across(s, step):
+        return pltpu.make_async_remote_copy(
+            src_ref=st.at[s], dst_ref=st.at[s + step], send_sem=ps_sem.at[s], recv_sem=sr_sem.at[s + step],
+            device_id=(lax.rem(me + N + step, N), mk), device_id_type=MESH,
+        )
+
+    def pieces_on(s, act):
+        @pl.when(jnp.logical_and(s + 2 <= W, me + 2 < N))
+        def _():
+            act(chain(s))
+
+        @pl.when(jnp.logical_and(odd == 0, s + 1 < W))
+        def _():
+            act(across(s, 1))
+
+        @pl.when(jnp.logical_and(odd == 1, jnp.logical_and(s >= 2, s - 1 < W)))
+        def _():
+            act(across(s, -1))
 
     def query(o):
         return pltpu.make_async_remote_copy(
@@ -119,11 +134,7 @@
             recv_sem=lr_sem.at[o], device_id=(lax.rem(me + N - o, N), mk), device_id_type=MESH,
         )
 
-    if W > 1:
-        @pl.when(me + 1 < N)
-        def _():
-            first_piece().start()
-
+    st[0] = skv_ref[...]
     def packed(o, kv):
         line = val[kv, pl.ds(lax.rem(me + o, N), 1), :]
         pick = one_hot(iota((RP, GT), 0) == line)
@@ -136,6 +147,7 @@
         return carry
 
     lax.fori_loop(1, N, send, 0)
+    pieces_on(0, lambda copy: copy.start())
     for kv in range(KV):
         qin[0, kv] = packed(0, kv)
 
@@ -173,27 +185,31 @@
         st[o] = jnp.zeros((2, T * KV, D), jnp.bfloat16)
         return carry
 
-    st[0] = skv_ref[...]
     lax.fori_loop(me + 1, W, blank, 0)
     serve(0, ain, lin)
 
     def turn(o, carry):
-        @pl.when(jnp.logical_and(o < W, o <= me))
-        def _():
-            piece(o - 1).wait_recv()
-
-            @pl.when(jnp.logical_and(o + 1 < W, me + 1 < N))
-            def _():
-                piece(o).start()
-
         query(o).wait_recv()
         serve(o, aout, lout)
         answer(o).start()
         answer_lse(o).start()
+
+        @pl.when(jnp.logical_and(lax.rem(o, 2) == 0, jnp.logical_and(o <= W, o <= me)))
+        def _():
+            chain(o - 2).wait_recv()
+            pieces_on(o, lambda copy: copy.start())
+
         return carry
 
     lax.fori_loop(1, N, turn, 0)
 
+    def landed(i, carry):
+        @pl.when(2 * i + 1 <= me)
+        def _():
+            across(2 * i, 1).wait_recv()
+        return carry
+
+    lax.fori_loop(0, W // 2, landed, 0)
     pt = 256 // (T * KV)
     c2 = iota((256, 256), 1)
     r2 = iota((256, 256), 0)
@@ -272,18 +288,14 @@
         return carry
 
     lax.fori_loop(1, N, drain, 0)
-    if W > 1:
-        @pl.when(me + 1 < N)
-        def _():
-            first_piece().wait_send()
-
-    def drain_piece(o, carry):
-        @pl.when(jnp.logical_and(o <= me, me + 1 < N))
-        def _():
-            piece(o).wait_send()
-        return carry
-
-    lax.fori_loop(1, W - 1, drain_piece, 0)
+
+    def drain_piece(i, carry):
+        @pl.when(2 * i <= me)
+        def _():
+            pieces_on(2 * i, lambda copy: copy.wait_send())
+        return carry
+
+    lax.fori_loop(0, min(W, N - 1) // 2 + 1, drain_piece, 0)
     own.wait()
     for j in range(1, KVH):
         part(j).wait()
@@ -323,7 +335,7 @@
             pltpu.VMEM((N, KV, RP, D), bf),
             pltpu.VMEM((N, 8, RL), f32),
             pltpu.VMEM((N, 8, RL), f32),
-            pltpu.VMEM((W, 2, T * KV, D), bf),
+            pltpu.VMEM((W + 2, 2, T * KV, D), bf),
             pltpu.VMEM((KV, W * T, D), bf),
             pltpu.VMEM((KV, W * T, 2 * D), bf),
             pltpu.VMEM((KV, G * T, 1), f32),
@@ -331,7 +343,7 @@
             pltpu.VMEM((KV, G * T, D), f32),
             pltpu.VMEM((T, H * D), bf),
             dma, dma((N,)), dma((N,)), dma((N,)), dma((N,)), dma((N,)), dma((N,)),
-            dma((W,)), dma((W,)), dma((KVH,)), dma((KVH,)),
+            dma((W + 2,)), dma((W + 2,)), dma((W + 2,)), dma((KVH,)), dma((KVH,)),
         ],
         compiler_params=pltpu.CompilerParams(
             collective_id=0, has_side_effects=True, vmem_limit_bytes=56 * 1024 * 1024

time: 73.3 us -> 68.1 us (0.929)
  Pallas kernels: 70 us -> 64.9 us
    pallas_call x1, Pallas kernels: 70 us -> 64.9 us  [per_device(): pl.pallas_call(functools.partial(kernel, cfg), out_shape=jax.ShapeDtypeSt...]
where the time goes in v4:
time: 68.1 us; the launch traced here: 68 us
  Pallas kernels  64.9 us (95%)
  local copies, waits for them, and re-layouts  3.09 us (5%)
    pallas_call x1, Pallas kernels, per_device(): pl.pallas_call(functools.partial(kernel, cfg), out_shape=jax.ShapeDtypeSt...  64.9 us
    unnamed x2, local copies, waits for them, and re-layouts  3.09 us

profile of v4, /device:TPU:1, one launch (start us, length us, event | category | flops | bytes accessed | tf_op | source)
XLA Modules:
  0.0 68.0 jit_solution(5258375739328347996)
XLA Ops:
  0.0 1.4 %copy.6.sel_ref = s32[2,64,3]{2,1,0:T(8,128)} copy(s32[2,64,3]{1,0,2:T(2,128)} %param.8) | data formatting | bytes 3072 | tf_op args[3]
  1.4 64.9 %shard_map.55 = bf16[16,8192]{1,0:T(8,128)(2,1)} custom-call(s32[2,64,3]{2,1,0:T(8,128)} %copy.6.sel_ref, s32[1,8]{1,0:T(1,128)} %bitcast.7, bf16[1024,128]{1,0:T(8,128)(2,1)} %bitcast.5, bf16[2,128,128]{2,1,0:T(8,128)(2,1)} %bitcast.6, bf16[2,4096,128]{2,1,0:T(8,128)(2,1)} %bitcast.4), custom_call_target="tpu_custom_call" | custom-call | flops 3489660928 | bytes 2097152 | tf_op jit(solution)/shard_map/pallas_call | solution.py:320
  66.3 1.7 %copy.8 = bf16[16,8192]{1,0:T(8,128)(2,1)} copy(bf16[16,8192]{1,0:T(8,128)(2,1)} %shard_map.55) | data formatting | bytes 524288

commit v5 on v4

--- a/solution.py
+++ b/solution.py
@@ -140,7 +140,11 @@
         pick = one_hot(iota((RP, GT), 0) == line)
         return dot(pick, qp[kv]).astype(jnp.bfloat16)
 
-    def send(o, carry):
+    def far(i):
+        return N // 2 + (i // 2) * (1 - 2 * lax.rem(i, 2))
+
+    def send(i, carry):
+        o = far(i)
         for kv in range(KV):
             qout[o, kv] = packed(o, kv)
         query(o).start()
@@ -188,16 +192,17 @@
     lax.fori_loop(me + 1, W, blank, 0)
     serve(0, ain, lin)
 
-    def turn(o, carry):
+    def turn(i, carry):
+        o = far(i)
         query(o).wait_recv()
         serve(o, aout, lout)
         answer(o).start()
         answer_lse(o).start()
 
-        @pl.when(jnp.logical_and(lax.rem(o, 2) == 0, jnp.logical_and(o <= W, o <= me)))
-        def _():
-            chain(o - 2).wait_recv()
-            pieces_on(o, lambda copy: copy.start())
+        @pl.when(jnp.logical_and(lax.rem(i, 2) == 0, jnp.logical_and(i <= W, i <= me)))
+        def _():
+            chain(i - 2).wait_recv()
+            pieces_on(i, lambda copy: copy.start())
 
         return carry
 
@@ -235,7 +240,9 @@
     lane = iota((GT, 128), 1)
     slot = iota((GT, RL), 1)
 
-    def merge(o, carry):
+    def merge(i, carry):
+        o = jnp.where(i == 0, 0, far(i))
+
         @pl.when(o > 0)
         def _():
             answer(o).wait_recv()

time: 68.1 us -> 67.2 us (0.987)
  the two profiles are of different devices: /device:TPU:1 before, /device:TPU:25 now
where the time goes in v5:
time: 67.2 us; the launch traced here: 67 us
  Pallas kernels  63.9 us (95%)
  local copies, waits for them, and re-layouts  3.09 us (5%)
    pallas_call x1, Pallas kernels, per_device(): pl.pallas_call(functools.partial(kernel, cfg), out_shape=jax.ShapeDtypeSt...  63.9 us
    unnamed x2, local copies, waits for them, and re-layouts  3.09 us

profile of v5, /device:TPU:25, one launch (start us, length us, event | category | flops | bytes accessed | tf_op | source)
XLA Modules:
  0.0 67.0 jit_solution(6878264094840058391)
XLA Ops:
  0.0 1.4 %copy.6.sel_ref = s32[2,64,3]{2,1,0:T(8,128)} copy(s32[2,64,3]{1,0,2:T(2,128)} %param.8) | data formatting | bytes 3072 | tf_op args[3]
  1.4 63.9 %shard_map.55 = bf16[16,8192]{1,0:T(8,128)(2,1)} custom-call(s32[2,64,3]{2,1,0:T(8,128)} %copy.6.sel_ref, s32[1,8]{1,0:T(1,128)} %bitcast.7, bf16[1024,128]{1,0:T(8,128)(2,1)} %bitcast.5, bf16[2,128,128]{2,1,0:T(8,128)(2,1)} %bitcast.6, bf16[2,4096,128]{2,1,0:T(8,128)(2,1)} %bitcast.4), custom_call_target="tpu_custom_call" | custom-call | flops 3489660928 | bytes 2097152 | tf_op jit(solution)/shard_map/pallas_call | solution.py:327
  65.3 1.7 %copy.8 = bf16[16,8192]{1,0:T(8,128)(2,1)} copy(bf16[16,8192]{1,0:T(8,128)(2,1)} %shard_map.55) | data formatting | bytes 524288
